TPU v7x, 256 devices: a whole 4x4x8 slice. The times are simulated.
256 devices in a mesh: blk: 32 (over x_hi, z, core), head: 8 (over x_lo, y).
Axes of the slice: x: 4 (x_hi: 2, x_lo: 2; x = x_hi * 2 + x_lo), y: 4, z: 8, core: 2. Of those that a mesh axis runs over, the one named last changes fastest.
Arguments:
- queries: bfloat16 [16384, 3072], P(('blk', 'head')), may hold values from -80 to 80
- keys: bfloat16 [16384, 3072], P(('blk', 'head')), may hold values from -9 to 9
- values: bfloat16 [16384, 3072], P(('blk', 'head')), may hold values from -6 to 6
- tile_mask: int32 [24, 128, 128], P('head', 'blk'), may hold values from 0 to 1, as said below
- out_weight: bfloat16 [3072, 3072], P('head'), may hold values from -0.109375 to 0.109375
Outputs:
- mixed: bfloat16 [16384, 3072], P(('blk', 'head'))
Inputs may be any that keep to these rules, and one draw needn't show every extreme that they name: `tile_mask`: every diagonal entry is 1.
All inputs are finite; a program needn't handle non-finite values.
Results may differ from a plain program's by a relative error of at most 0.014.
Values may be sent and summed in bfloat16 or wider, within the bound.
A program may use at most 192 MiB of HBM per device.

v0:
```python
import math

import jax
import jax.numpy as jnp
from jax import lax
from jax.sharding import PartitionSpec as P

HEAD_DIM = 128
TILE = 128


def body(queries, keys, values, tile_mask, out_weight):
    query_local, key_local, value_local = (
        lax.all_to_all(queries, "head", split_axis=1, concat_axis=0, tiled=True),
        lax.all_to_all(keys, "head", split_axis=1, concat_axis=0, tiled=True),
        lax.all_to_all(values, "head", split_axis=1, concat_axis=0, tiled=True),
    )
    row_count = query_local.shape[0]
    heads_here = query_local.shape[1] // HEAD_DIM
    row_tiles = row_count // TILE
    query_heads = query_local.reshape(row_count, heads_here, HEAD_DIM).transpose(1, 0, 2)
    score_scale = 1.0 / math.sqrt(HEAD_DIM)
    start_state = (
        jnp.full((heads_here, row_count), -1e30, jnp.float32),
        jnp.zeros((heads_here, row_count), jnp.float32),
        jnp.zeros((heads_here, row_count, HEAD_DIM), jnp.float32),
    )
    key_piece = lax.all_gather(key_local, "blk", axis=0, tiled=True)
    value_piece = lax.all_gather(value_local, "blk", axis=0, tiled=True)
    piece_rows = key_piece.shape[0]
    block_width = min(piece_rows, row_count)
    block_steps = piece_rows // block_width
    col_tiles = block_width // TILE
    key_blocks = key_piece.reshape(block_steps, block_width, heads_here, HEAD_DIM)
    value_blocks = value_piece.reshape(block_steps, block_width, heads_here, HEAD_DIM)
    block_starts = jnp.arange(block_steps, dtype=jnp.int32) * block_width

    def attend_block(state_now, block_in):
        key_block, value_block, first_key = block_in
        running_top, running_total, running_sum = state_now
        scores = (
            jnp.einsum("hqd,khd->hqk", query_heads, key_block, preferred_element_type=jnp.float32)
            * score_scale
        )
        mask_tiles = lax.dynamic_slice_in_dim(tile_mask, first_key // TILE, col_tiles, 2) > 0
        tiled = scores.reshape(heads_here, row_tiles, TILE, col_tiles, TILE)
        tile_allowed = mask_tiles[:, :, None, :, None]
        tiled = jnp.where(tile_allowed, tiled, -1e30)
        next_top = jnp.maximum(
            running_top, jnp.max(tiled, axis=(3, 4)).reshape(heads_here, row_count)
        )
        shifted = tiled - next_top.reshape(heads_here, row_tiles, TILE)[:, :, :, None, None]
        weights = jnp.where(tile_allowed, jnp.exp(shifted), 0.0).reshape(
            heads_here, row_count, block_width
        )
        shrink = jnp.exp(running_top - next_top)
        next_total = running_total * shrink + jnp.sum(weights, axis=2)
        next_sum = running_sum * shrink[:, :, None] + jnp.einsum(
            "hqk,khd->hqd",
            weights.astype(jnp.bfloat16),
            value_block,
            preferred_element_type=jnp.float32,
        )
        return ((next_top, next_total, next_sum), None)

    state_out, unused = lax.scan(
        attend_block, start_state, (key_blocks, value_blocks, block_starts)
    )
    final_top, final_total, final_sum = state_out
    attention = (
        (final_sum / final_total[:, :, None])
        .transpose(1, 0, 2)
        .reshape(row_count, heads_here * HEAD_DIM)
        .astype(jnp.bfloat16)
    )
    token_side = lax.all_to_all(attention, "head", split_axis=0, concat_axis=1, tiled=True)
    mixed = jnp.dot(
        token_side,
        lax.all_gather(out_weight, "head", axis=0, tiled=True),
        preferred_element_type=jnp.float32,
    )
    return mixed.astype(jnp.bfloat16)


def solution(mesh):
    placed = (
        P(("blk", "head"), None),
        P(("blk", "head"), None),
        P(("blk", "head"), None),
        P("head", "blk", None),
        P("head", None),
    )
    return jax.shard_map(
        body, mesh=mesh, in_specs=placed, out_specs=P(("blk", "head"), None), check_vma=False
    )
```

profile of v0, /device:TPU:1, one launch (start us, length us, event | category | flops | bytes accessed | tf_op | source)
XLA Modules:
  0.0 864.2 jit_solution(4054754925960821868)
XLA Ops:
  7.6 13.3 %all_to_all.70 = bf16[64,8,384]{2,0,1:T(8,128)(2,1)} all-to-all(bf16[64,8,384]{2,0,1:T(8,128)(2,1)S(1)} %bitcast.72), channel_id=1, replica_groups=mesh['blk'=32,'head'=8] {'head'}, dimensions={1} | all-to-all | bytes 786432 | tf_op jit(solution)/shard_map/all_to_all | solution.py:15
  22.0 9.9 %all_to_all.71 = bf16[64,8,384]{2,0,1:T(8,128)(2,1)} all-to-all(bf16[64,8,384]{2,0,1:T(8,128)(2,1)S(1)} %bitcast.73), channel_id=1, replica_groups=mesh['blk'=32,'head'=8] {'head'}, dimensions={1} | all-to-all | bytes 786432 | tf_op jit(solution)/shard_map/all_to_all | solution.py:16
  32.8 3.5 all-to-all-start.1
  37.5 8.6 all-to-all-done.1
  46.3 95.8 %all-gather.4.cloned.1.call-done = bf16[16384,384]{1,0:T(8,128)(2,1)} async-done(((bf16[512,384]{1,0:T(8,128)(2,1)}), bf16[16384,384]{1,0:T(8,128)(2,1)}) %all-gather.4.cloned.1.call-update) | async-done | bytes 12582928 | tf_op jit(solution)/shard_map/all_gather | solution.py:28
  142.1 32.2 %reshape.48 = bf16[32,512,3,128]{3,2,1,0:T(4,128)(2,1)} reshape(bf16[16384,384]{1,0:T(8,128)(2,1)} %all-gather.4.cloned.1.call-done) | data formatting | bytes 25165824 | tf_op jit(solution)/shard_map/reshape | solution.py:34
  174.2 13.0 %copy.37 = bf16[32,512,3,128]{3,1,2,0:T(8,128)(2,1)} copy(bf16[32,512,3,128]{3,2,1,0:T(4,128)(2,1)} %reshape.48) | data formatting | bytes 25165824
  187.2 71.9 %all-gather.6.cloned.1.call-done = bf16[16384,384]{1,0:T(8,128)(2,1)} async-done(((bf16[512,384]{1,0:T(8,128)(2,1)}), bf16[16384,384]{1,0:T(8,128)(2,1)}) %all-gather.6.cloned.1.call-update) | async-done | bytes 12582928 | tf_op jit(solution)/shard_map/all_gather | solution.py:29
  259.1 32.2 %reshape.49 = bf16[32,512,3,128]{3,2,1,0:T(4,128)(2,1)} reshape(bf16[16384,384]{1,0:T(8,128)(2,1)} %all-gather.6.cloned.1.call-done) | data formatting | bytes 25165824 | tf_op jit(solution)/shard_map/reshape | solution.py:35
  291.3 13.0 %copy.39 = bf16[32,512,3,128]{3,1,2,0:T(8,128)(2,1)} copy(bf16[32,512,3,128]{3,2,1,0:T(4,128)(2,1)} %reshape.49) | data formatting | bytes 25165824
  304.3 529.0 %while.17 = (s32[]{:T(128)}, f32[3,512]{1,0:T(4,128)S(1)}, f32[3,512]{1,0:T(4,128)}, f32[3,512,128]{2,1,0:T(8,128)}, s32[32]{0:T(128)}, /*index=5*/s32[3,4,128]{...) while((s32[]{:T(128)}, f32[3,512]{1,0:T(4,128)S(1)}, ...), condition=%wide.region_3.4_spmd.clone, body=%wide.region_0.3_spmd.clone.sunk | while | flops 413474368 | bytes 26495500 | solution.py:66
  317.3 2.6 fusion.36
  330.6 2.7 fusion.34
  333.9 2.6 fusion.36
  350.4 2.6 fusion.36
  363.7 2.7 fusion.34
  367.0 2.6 fusion.36
  380.3 2.6 fusion.34
  383.5 2.6 fusion.36
  400.1 2.6 fusion.36
  413.4 2.7 fusion.34
  416.7 2.6 fusion.36
  433.2 2.6 fusion.36
  449.7 2.6 fusion.36
  466.2 2.6 fusion.36
  482.8 2.6 fusion.36
  499.3 2.6 fusion.36
  515.8 2.6 fusion.36
  532.3 2.6 fusion.36
  548.8 2.6 fusion.36
  565.4 2.6 fusion.36
  581.9 2.6 fusion.36
  598.4 2.6 fusion.36
  614.9 2.6 fusion.36
  631.5 2.6 fusion.36
  648.0 2.6 fusion.36
  664.5 2.6 fusion.36
  681.0 2.6 fusion.36
  697.5 2.6 fusion.36
  714.1 2.6 fusion.36
  730.6 2.6 fusion.36
  747.1 2.6 fusion.36
  763.6 2.6 fusion.36
  780.2 2.6 fusion.36
  796.7 2.6 fusion.36
  829.7 2.6 fusion.36
  835.3 11.8 %all_to_all.72 = bf16[8,64,384]{2,1,0:T(8,128)(2,1)S(1)} all-to-all(bf16[8,64,384]{2,1,0:T(8,128)(2,1)S(1)} %convert_element_type.21), channel_id=1, replica_groups=mesh['blk'=32,'head'=8] {'head'}, dimensions={0} | all-to-all | bytes 786432 | tf_op jit(solution)/shard_map/all_to_all | solution.py:76
  847.2 10.5 %convolution_convert_fusion = bf16[64,3072]{1,0:T(8,128)(2,1)} fusion(bf16[64,3072]{1,0:T(8,128)(2,1)S(1)} %bitcast.66, bf16[3072,3072]{1,0:T(8,128)(2,1)} %all-gather.8.cloned.1.call-done), kind=kOutput, calls=%fused_computation.24 | convolution fusion | flops 1208156160 | bytes 19660800 | tf_op jit(solution)/shard_map/dot_general | solution.py:77
  (691 shorter events, 357.0 us)
Async XLA Ops:
  6.5 25.4 %copy-start.3 = (bf16[64,3072]{1,0:T(8,128)(2,1)S(1)}, bf16[64,3072]{1,0:T(8,128)(2,1)}, u32[]{:S(2)}) copy-start(bf16[64,3072]{1,0:T(8,128)(2,1)} %param.7) | copy-start | bytes 1179652
  6.5 135.5 %all-gather.4.cloned.1.call-start = ((), (), s32[]{:S(2)}) async-start(), calls=%async_computation.4 | async-start | bytes 12976128 | tf_op jit(solution)/shard_map/all_gather | solution.py:28
  20.9 238.2 %all-gather.6.cloned.1.call-start = ((), (), s32[]{:S(2)}) async-start(), calls=%async_computation.5 | async-start | bytes 12976128 | tf_op jit(solution)/shard_map/all_gather | solution.py:29
  32.8 13.3 %all-to-all-start.1 = ((bf16[64,8,384]{2,0,1:T(8,128)(2,1)}), bf16[64,8,384]{2,0,1:T(8,128)(2,1)S(1)}, u32[]{:S(2)}, u32[]{:S(2)}) async-start(bf16[64,8,384]{2,0,1:T(8,128)(2,1)} %bitcast.50), calls=%async_computation.1 | async-start | bytes 786432 | tf_op jit(solution)/shard_map/all_to_all | solution.py:14
  36.2 811.0 %all-gather.8.cloned.1.call-start = ((), (), s32[]{:S(2)}) async-start(), calls=%async_computation.6 | async-start | bytes 21233664 | tf_op jit(solution)/shard_map/all_gather | solution.py:79
  314.0 3.3 copy-start
  314.0 3.3 copy-start.1
  330.5 3.3 copy-start
  330.5 3.3 copy-start.1
  347.1 3.3 copy-start
  347.1 3.3 copy-start.1
  363.7 3.3 copy-start
  363.7 3.3 copy-start.1
  380.2 3.3 copy-start
  380.2 3.3 copy-start.1
  396.8 3.3 copy-start
  396.8 3.3 copy-start.1
  413.3 3.3 copy-start
  413.3 3.3 copy-start.1
  429.9 3.3 copy-start
  429.9 3.3 copy-start.1
  446.4 3.3 copy-start
  446.4 3.3 copy-start.1
  462.9 3.3 copy-start
  462.9 3.3 copy-start.1
  479.5 3.3 copy-start
  496.0 3.3 copy-start
  512.5 3.3 copy-start
  512.5 3.3 copy-start.1
  529.0 3.3 copy-start
  545.5 3.3 copy-start
  562.1 3.3 copy-start
  578.6 3.3 copy-start
  595.1 3.3 copy-start
  611.6 3.3 copy-start
  628.2 3.3 copy-start
  644.7 3.3 copy-start
  661.2 3.3 copy-start
  677.7 3.3 copy-start
  694.2 3.3 copy-start
  710.8 3.3 copy-start
  727.3 3.3 copy-start
  743.8 3.3 copy-start
  760.3 3.3 copy-start
  776.9 3.3 copy-start
  793.4 3.3 copy-start
  809.9 3.3 copy-start
  826.4 3.3 copy-start
  (117 other events, 202.2 us)
Sparse Core Ops, SparseCore 0:
  21.0 120.9 all-gather.3
  144.8 114.2 all-gather.5
  260.9 189.2 all-gather.7
where the time goes:
time: 871 us; the launch traced here: 864 us
  local copies, waits for them, and re-layouts  305 us (35%)
  waiting for transfers between devices  177 us (20%)
  matrix products  157 us (18%)
  other arithmetic  87.2 us (10%)
  loops' own time  86.4 us (10%)
  blocking collectives  35 us (4%)
  between operations  13.2 us (2%)
    broadcast_in_dim x64, local copies, waits for them, and re-layouts, attend_block(): tiled = jnp.where(tile_allowed, tiled, -1e+30)  97.7 us
    all_gather x1, waiting for transfers between devices, body(): key_piece = lax.all_gather(key_local, 'blk', axis=0, tiled=True)  95.8 us
    another operation x1, loops' own time, body(): lax.scan(attend_block, start_state, (key_blocks, value_blocks, block_star...  86.4 us
    reduce_sum x32, other arithmetic, attend_block(): next_total = running_total * shrink + jnp.sum(weights, axis=2)  84.2 us
    dot_general x32, matrix products, attend_block(): jnp.einsum('hqk,khd->hqd', weights.astype(jnp.bfloat16), value_block, pre...  84.1 us
    all_gather x1, waiting for transfers between devices, body(): value_piece = lax.all_gather(value_local, 'blk', axis=0, tiled=True)  71.9 us
    dot_general x32, matrix products, attend_block(): jnp.einsum('hqd,khd->hqk', query_heads, key_block, preferred_element_type...  62.3 us
    while x352, local copies, waits for them, and re-layouts  47.4 us
  transfers between devices with their start and end apart: 4, of which 3 were waited for; matrix products, arithmetic and copies ran while one was open for 57% of the time, Pallas kernels for 0%

commit v1 on v0

v1 whole, which is shorter than its diff:
```python
import functools
import math

import jax
import jax.numpy as jnp
from jax import lax
from jax.experimental import pallas as pl
from jax.experimental.pallas import tpu as pltpu
from jax.sharding import PartitionSpec as P

HEAD_DIM = 128
TILE = 128
MESH = pl.DeviceIdType.MESH
TO_LOG2 = math.log2(math.e) / math.sqrt(HEAD_DIM)
LOW = -1e30
BLOCKED = 2e30
VMEM_LIMIT = 60 * 2**20
NX, NY, NZ = 2, 4, 8


def place():
    blk, head = lax.axis_index("blk"), lax.axis_index("head")
    return blk // 16, (blk // 2) % NZ, blk % 2, head // NY, head % NY


def at(x_hi, z, core, x_lo, y):
    return (x_hi * 16 + z * 2 + core, x_lo * NY + y)


def greet(peers):
    barrier = pltpu.get_barrier_semaphore()
    for peer in peers:
        pl.semaphore_signal(barrier, inc=1, device_id=peer, device_id_type=MESH)
    pl.semaphore_wait(barrier, len(peers))


class Wires:
    def __init__(self, send_sems, recv_sems, local_sems):
        self.send_sems, self.recv_sems, self.local_sems = send_sems, recv_sems, local_sems
        self.used, self.used_local = 0, 0
        self.sent = []

    def push(self, src, dst, peer, land=None):
        copy = pltpu.make_async_remote_copy(
            src_ref=src,
            dst_ref=dst,
            send_sem=self.send_sems.at[self.used],
            recv_sem=self.recv_sems.at[self.used],
            device_id=peer,
            device_id_type=MESH,
        )
        arrival = copy
        if land is not None:
            arrival = pltpu.make_async_remote_copy(
                src_ref=land,
                dst_ref=land,
                send_sem=self.send_sems.at[self.used],
                recv_sem=self.recv_sems.at[self.used],
                device_id=peer,
                device_id_type=MESH,
            )
        self.used += 1
        copy.start()
        self.sent.append(copy)
        return arrival

    def local(self, src, dst):
        copy = pltpu.make_async_copy(src, dst, self.local_sems.at[self.used_local])
        self.used_local += 1
        copy.start()
        return copy

    def finish(self):
        for copy in self.sent:
            copy.wait_send()


def spread_kernel(q, k, v, m, w, q_all, k_all, v_all, m_all, w_all, send_sems, recv_sems, local_sems):
    x_hi, z, core, x_lo, y = place()
    rows = q.shape[0]
    width = q_all.shape[2]
    group = x_lo * NY + y
    other_hi, other_core, other_lo = 1 - x_hi, 1 - core, 1 - x_lo
    slot = x_hi * 2 + core
    sibling = at(x_hi, z, other_core, x_lo, y)
    across = at(other_hi, z, core, x_lo, y)
    diagonal = at(other_hi, z, other_core, x_lo, y)
    z_up, z_down = (z + 1) % NZ, (z + NZ - 1) % NZ
    up, down = at(x_hi, z_up, core, x_lo, y), at(x_hi, z_down, core, x_lo, y)
    y_up, y_down, y_far = (y + 1) % NY, (y + NY - 1) % NY, (y + 2) % NY
    partner = at(x_hi, z, core, other_lo, y)
    outer = at(other_hi, z, core, other_lo, y)
    blk = x_hi * 16 + z * 2 + core
    head_peers = [(group + step) % 8 for step in range(1, 8)]
    greet([(blk, peer) for peer in head_peers] + [sibling, across, diagonal, up, down, outer])
    wires = Wires(send_sems, recv_sems, local_sems)

    def exchange(src, dst_slot):
        arrivals = []
        for step in range(1, 8):
            peer = (group + step) % 8
            origin = (group + 8 - step) % 8
            arrivals.append(
                wires.push(
                    src.at[:, pl.ds(pl.multiple_of(peer * width, 128), width)],
                    dst_slot.at[pl.ds(pl.multiple_of(group * rows, 64), rows), :],
                    (blk, peer),
                    dst_slot.at[pl.ds(pl.multiple_of(origin * rows, 64), rows), :],
                )
            )
        own = wires.local(
            src.at[:, pl.ds(pl.multiple_of(group * width, 128), width)],
            dst_slot.at[pl.ds(pl.multiple_of(group * rows, 64), rows), :],
        )
        return arrivals, own

    def settle(pending):
        for arrival in pending[0]:
            arrival.wait_recv()
        pending[1].wait()

    k_wait = exchange(k, k_all.at[z])
    v_wait = exchange(v, v_all.at[z])
    q_wait = exchange(q, q_all.at[slot])
    m_wait = [
        wires.push(m, m_all.at[slot], sibling, m_all.at[x_hi * 2 + other_core]),
        wires.push(m, m_all.at[slot], across, m_all.at[other_hi * 2 + core]),
        wires.push(m, m_all.at[slot], diagonal, m_all.at[other_hi * 2 + other_core]),
    ]
    m_own = wires.local(m, m_all.at[slot])
    w_own = wires.local(w, w_all.at[group])

    def ring_step(full, step, direction):
        if direction > 0:
            held = (z + NZ - step) % NZ
            landing = (z + NZ - step - 1) % NZ
            return wires.push(full.at[held], full.at[held], up, full.at[landing])
        held = (z + step) % NZ
        landing = (z + step + 1) % NZ
        return wires.push(full.at[held], full.at[held], down, full.at[landing])

    settle(k_wait)
    ring = {}
    ring["ku"] = ring_step(k_all, 0, 1)
    ring["kd"] = ring_step(k_all, 0, -1)
    settle(v_wait)
    ring["vu"] = ring_step(v_all, 0, 1)
    ring["vd"] = ring_step(v_all, 0, -1)

    depth = w.shape[0]
    half = depth // 2
    columns = w.shape[1] // 2
    mine = pl.ds(pl.multiple_of(core * columns, 128), columns)
    theirs = pl.ds(pl.multiple_of(other_core * columns, 128), columns)
    top, bottom = pl.ds(0, half), pl.ds(half, half)

    def w_part(lo, yy, part, cols):
        return w_all.at[lo * NY + yy, part, cols]

    whole = pl.ds(0, depth)
    w_up = wires.push(w.at[:, mine], w_part(x_lo, y, whole, mine), (blk, x_lo * NY + y_up), w_part(x_lo, y_down, whole, mine))
    w_down = wires.push(w.at[:, mine], w_part(x_lo, y, whole, mine), (blk, x_lo * NY + y_down), w_part(x_lo, y_up, whole, mine))

    def w_cross(yy):
        return (
            wires.push(w_part(x_lo, yy, top, mine), w_part(x_lo, yy, top, mine), partner, w_part(other_lo, yy, top, mine)),
            wires.push(w_part(x_lo, yy, bottom, mine), w_part(x_lo, yy, bottom, mine), outer, w_part(other_lo, yy, bottom, mine)),
        )

    tail = []

    def w_swap(lo, yy, part):
        tail.append(wires.push(w_part(lo, yy, part, mine), w_part(lo, yy, part, mine), sibling, w_part(lo, yy, part, theirs)))

    settle(q_wait)
    tail.append(wires.push(q_all.at[slot], q_all.at[slot], sibling, q_all.at[x_hi * 2 + other_core]))
    q_across = wires.push(q_all.at[slot], q_all.at[slot], across, q_all.at[other_hi * 2 + core])
    w_own.wait()
    crossing = [w_cross(y)]

    q_across.wait_recv()
    tail.append(
        wires.push(
            q_all.at[other_hi * 2 + core],
            q_all.at[other_hi * 2 + core],
            sibling,
            q_all.at[other_hi * 2 + other_core],
        )
    )

    def ring_turn(step):
        for key, full in (("k", k_all), ("v", v_all)):
            for tag, direction in (("u", 1), ("d", -1)):
                name = key + tag
                if name not in ring:
                    continue
                ring[name].wait_recv()
                last = 4 if name in ("ku", "vd") else 3
                if step < last:
                    ring[name] = ring_step(full, step, direction)
                else:
                    del ring[name]

    ring_turn(1)
    w_up.wait_recv()
    w_far_up = wires.push(
        w_part(x_lo, y_down, top, mine), w_part(x_lo, y_down, top, mine), (blk, x_lo * NY + y_up), w_part(x_lo, y_far, top, mine)
    )
    crossing.append(w_cross(y_down))
    w_swap(x_lo, y_down, whole)
    w_down.wait_recv()
    w_far_down = wires.push(
        w_part(x_lo, y_up, bottom, mine), w_part(x_lo, y_up, bottom, mine), (blk, x_lo * NY + y_down), w_part(x_lo, y_far, bottom, mine)
    )
    crossing.append(w_cross(y_up))
    w_swap(x_lo, y_up, whole)

    def crossed(index, yy):
        crossing[index][0].wait_recv()
        w_swap(other_lo, yy, top)
        crossing[index][1].wait_recv()
        w_swap(other_lo, yy, bottom)

    crossed(0, y)
    ring_turn(2)
    w_far_up.wait_recv()
    w_far_down.wait_recv()
    crossing.append(w_cross(y_far))
    w_swap(x_lo, y_far, whole)
    crossed(1, y_down)
    crossed(2, y_up)
    ring_turn(3)
    crossed(3, y_far)
    ring_turn(4)
    for arrival in tail + m_wait:
        arrival.wait_recv()
    m_own.wait()
    wires.finish()


def spread(q, k, v, m, w):
    rows = q.shape[0]
    width = q.shape[1] // 8
    slab = rows * 8
    hbm = pl.BlockSpec(memory_space=pl.ANY)
    return pl.pallas_call(
        spread_kernel,
        out_shape=[
            jax.ShapeDtypeStruct((4, slab, width), q.dtype),
            jax.ShapeDtypeStruct((NZ, slab, width), k.dtype),
            jax.ShapeDtypeStruct((NZ, slab, width), v.dtype),
            jax.ShapeDtypeStruct((4,) + m.shape, m.dtype),
            jax.ShapeDtypeStruct((8,) + w.shape, w.dtype),
        ],
        in_specs=[hbm] * 5,
        out_specs=[hbm] * 5,
        scratch_shapes=[
            pltpu.SemaphoreType.DMA((80,)),
            pltpu.SemaphoreType.DMA((80,)),
            pltpu.SemaphoreType.DMA((8,)),
        ],
        name="spread",
        compiler_params=pltpu.CompilerParams(collective_id=1, has_side_effects=True),
    )(q, k, v, m, w)


def attend_kernel(bias, q_ref, k_ref, v_ref, o_ref, stat_ref, acc, v_turned):
    heads = bias.shape[0]
    q_count, k_count = q_ref.shape[0], k_ref.shape[0]
    step_keys = 512
    steps = k_count // step_keys
    tiles = step_keys // TILE
    slots, slot_rows = o_ref.shape[0], o_ref.shape[2]
    stat_ref[...] = jnp.zeros_like(stat_ref)
    ones = jnp.ones((16, step_keys), jnp.bfloat16)

    for head in range(heads):
        lanes = pl.ds(head * HEAD_DIM, HEAD_DIM)

        def turn(i, unused):
            at_keys = pl.ds(pl.multiple_of(i * step_keys, step_keys), step_keys)
            v_turned[:, at_keys] = v_ref[at_keys, lanes].T
            return unused

        lax.fori_loop(0, steps, turn, 0)
        scaled = q_ref[:, lanes].astype(jnp.float32) * TO_LOG2
        coarse = scaled.astype(jnp.bfloat16)
        fine = (scaled - coarse.astype(jnp.float32)).astype(jnp.bfloat16)
        query = jnp.concatenate([coarse, fine], axis=1)
        acc[...] = jnp.zeros_like(acc)

        def step(i, carry):
            top, total = carry
            at_keys = pl.ds(pl.multiple_of(i * step_keys, step_keys), step_keys)
            key = k_ref[at_keys, lanes]
            scores = lax.dot_general(
                jnp.concatenate([key, key], axis=1),
                query,
                (((1,), (1,)), ((), ())),
                preferred_element_type=jnp.float32,
            )
            blocked = [bias[head, pl.ds(i * tiles + a, 1), :] for a in range(tiles)]
            next_top = top
            for a in range(tiles):
                tile_top = jnp.max(scores[a * TILE : (a + 1) * TILE], axis=0, keepdims=True)
                next_top = jnp.maximum(next_top, tile_top - blocked[a])
            weights = jnp.concatenate(
                [
                    jnp.exp2(scores[a * TILE : (a + 1) * TILE] - (next_top + blocked[a])).astype(jnp.bfloat16)
                    for a in range(tiles)
                ],
                axis=0,
            )
            shrink = jnp.exp2(top - next_top)
            added = lax.dot_general(
                jnp.concatenate([v_turned[:, at_keys], ones], axis=0),
                weights,
                (((1,), (0,)), ((), ())),
                preferred_element_type=jnp.float32,
            )
            acc[...] = acc[...] * shrink + added[:HEAD_DIM]
            return next_top, total * shrink + added[HEAD_DIM : HEAD_DIM + 1]

        start = (jnp.full((1, q_count), LOW, jnp.float32), jnp.zeros((1, q_count), jnp.float32))
        top, total = lax.fori_loop(0, steps, step, start, unroll=2)
        mean = (acc[...] / jnp.maximum(total, 1e-30)).astype(jnp.bfloat16)
        for s in range(slots):
            cols = slice(s * slot_rows, (s + 1) * slot_rows)
            o_ref[s, head * HEAD_DIM : (head + 1) * HEAD_DIM, :] = mean[:, cols]
            stat_ref[s, head : head + 1, :] = top[:, cols]
            stat_ref[s, 3 + head : 4 + head, :] = total[:, cols]


def attend(bias, q_all, k_all, v_all):
    slots, slab, width = q_all.shape
    vmem = pl.BlockSpec(memory_space=pltpu.VMEM)
    q_count, k_count = slots * slab, k_all.shape[0] * slab
    return pl.pallas_call(
        attend_kernel,
        out_shape=[
            jax.ShapeDtypeStruct((slots, width, slab), jnp.bfloat16),
            jax.ShapeDtypeStruct((slots, 8, slab), jnp.float32),
        ],
        in_specs=[vmem] * 4,
        out_specs=[vmem] * 2,
        scratch_shapes=[
            pltpu.VMEM((HEAD_DIM, q_count), jnp.float32),
            pltpu.VMEM((HEAD_DIM, k_count), jnp.bfloat16),
        ],
        name="attend",
        compiler_params=pltpu.CompilerParams(vmem_limit_bytes=VMEM_LIMIT),
    )(bias, q_all.reshape(q_count, width), k_all.reshape(k_count, width), v_all.reshape(k_count, width))


def merge_kernel(o, stat, w, out, o_in, stat_in, mixed_in, ready, w_here, send_sems, recv_sems, local_sems):
    x_hi, z, core, x_lo, y = place()
    group = x_lo * NY + y
    other_hi, other_core = 1 - x_hi, 1 - core
    slot = x_hi * 2 + core
    blk = x_hi * 16 + z * 2 + core
    rows = out.shape[0]
    heads = 3
    wires = Wires(send_sems, recv_sems, local_sems)
    w_loads = [wires.local(w.at[g], w_here.at[g]) for g in range(8)]
    others = [(other_hi, core), (other_hi, other_core), (x_hi, other_core)]
    greet(
        [(blk, (group + step) % 8) for step in range(1, 8)]
        + [at(hi, z, c, x_lo, y) for hi, c in others]
    )
    arrivals = []
    for hi, c in others:
        peer_slot, peer = hi * 2 + c, at(hi, z, c, x_lo, y)
        arrivals.append(wires.push(o.at[peer_slot], o_in.at[slot], peer, o_in.at[peer_slot]))
        arrivals.append(wires.push(stat.at[peer_slot], stat_in.at[slot], peer, stat_in.at[peer_slot]))
    for arrival in arrivals:
        arrival.wait_recv()
    o_in[slot] = o[slot]
    stat_in[slot] = stat[slot]
    slots = o_in.shape[0]
    for head in range(heads):
        tops = [stat_in[s, head : head + 1, :] for s in range(slots)]
        best = functools.reduce(jnp.maximum, tops)
        shares = [stat_in[s, 3 + head : 4 + head, :] * jnp.exp2(tops[s] - best) for s in range(slots)]
        total = functools.reduce(jnp.add, shares)
        band = slice(head * HEAD_DIM, (head + 1) * HEAD_DIM)
        blend = functools.reduce(
            jnp.add,
            [o_in[s, band, :].astype(jnp.float32) * (shares[s] / total) for s in range(slots)],
        )
        ready[:, band] = blend.T.astype(jnp.bfloat16)
    pieces = []
    for step in range(1, 8):
        peer = (group + step) % 8
        origin = (group + 8 - step) % 8
        pieces.append(
            wires.push(
                ready.at[pl.ds(pl.multiple_of(peer * rows, 64), rows), :],
                mixed_in.at[group],
                (blk, peer),
                mixed_in.at[origin],
            )
        )
    mixed_in[group] = ready[pl.ds(pl.multiple_of(group * rows, 64), rows), :]
    for piece in pieces:
        piece.wait_recv()
    for load in w_loads:
        load.wait()
    cols = 768
    for c in range(out.shape[1] // cols):
        total = jnp.zeros((rows, cols), jnp.float32)
        for g in range(8):
            total += jnp.dot(
                mixed_in[g], w_here[g, :, c * cols : (c + 1) * cols], preferred_element_type=jnp.float32
            )
        out[:, c * cols : (c + 1) * cols] = total.astype(jnp.bfloat16)
    wires.finish()


def merge(o, stat, w_all, rows):
    slots, width, slab = o.shape
    vmem = pl.BlockSpec(memory_space=pltpu.VMEM)
    return pl.pallas_call(
        merge_kernel,
        out_shape=jax.ShapeDtypeStruct((rows, w_all.shape[2]), jnp.bfloat16),
        in_specs=[vmem, vmem, pl.BlockSpec(memory_space=pl.ANY)],
        out_specs=vmem,
        scratch_shapes=[
            pltpu.VMEM(o.shape, o.dtype),
            pltpu.VMEM(stat.shape, stat.dtype),
            pltpu.VMEM((8, rows, width), jnp.bfloat16),
            pltpu.VMEM((slab, width), jnp.bfloat16),
            pltpu.VMEM(w_all.shape, w_all.dtype),
            pltpu.SemaphoreType.DMA((16,)),
            pltpu.SemaphoreType.DMA((16,)),
            pltpu.SemaphoreType.DMA((8,)),
        ],
        name="merge",
        compiler_params=pltpu.CompilerParams(
            collective_id=2, has_side_effects=True, vmem_limit_bytes=VMEM_LIMIT
        ),
    )(o, stat, w_all)


def body(queries, keys, values, tile_mask, out_weight):
    x_hi, z, core, x_lo, y = place()
    q_all, k_all, v_all, m_all, w_all = spread(queries, keys, values, tile_mask, out_weight)
    slots, heads, row_tiles, tiles = m_all.shape
    by_place = m_all.reshape(slots, heads, row_tiles, 2, NZ, 2, row_tiles)
    here = lax.dynamic_index_in_dim(by_place, x_hi, 3, keepdims=False)
    here = lax.dynamic_index_in_dim(here, core, 4, keepdims=False)
    here = here.transpose(1, 3, 4, 0, 2).reshape(heads, NZ * row_tiles, slots * row_tiles)
    bias = jnp.repeat(jnp.where(here > 0, 0.0, BLOCKED).astype(jnp.float32), TILE, axis=2)
    o, stat = attend(bias, q_all, k_all, v_all)
    return merge(o, stat, w_all, queries.shape[0])


def solution(mesh):
    placed = (
        P(("blk", "head"), None),
        P(("blk", "head"), None),
        P(("blk", "head"), None),
        P("head", "blk", None),
        P("head", None),
    )
    return jax.shard_map(
        body, mesh=mesh, in_specs=placed, out_specs=P(("blk", "head"), None), check_vma=False
    )
```

time: 871 us -> 223 us (0.26)
  local copies, waits for them, and re-layouts: 305 us -> 5.79 us
  Pallas kernels: 0 us -> 217 us
  waiting for transfers between devices: 177 us -> 0 us
  matrix products: 157 us -> 0 us
  other arithmetic: 87.2 us -> 0.26 us
  loops' own time: 86.4 us -> 0 us
  blocking collectives: 35 us -> 0 us
  between operations: 13.2 us -> 0.04 us
    pallas_call x0 -> x3, Pallas kernels: none -> 217 us  [the longest x1 142 us: spread(): pl.pallas_call(spread_kernel, out_shape=[jax.ShapeDtypeStruct((4, slab, w...]
    all_gather x3 -> x0, waiting for transfers between devices: 168 us -> none  [the longest x1 95.8 us: body(): key_piece = lax.all_gather(key_local, 'blk', axis=0, tiled=True)]
    dot_general x65 -> x0, matrix products: 157 us -> none  [the longest x32 84.1 us: attend_block(): jnp.einsum('hqk,khd->hqd', weights.astype(jnp.bfloat16), value_block, pre...]
    broadcast_in_dim x64 -> x1, local copies, waits for them, and re-layouts: 97.7 us -> 0.27 us  [body(): jnp.repeat(jnp.where(here > 0, 0.0, BLOCKED).astype(jnp.float32), TILE, a...]
    another operation x1 -> x0, loops' own time: 86.4 us -> none  [body(): lax.scan(attend_block, start_state, (key_blocks, value_blocks, block_star...]
    reduce_sum x32 -> x0, other arithmetic: 84.2 us -> none  [attend_block(): next_total = running_total * shrink + jnp.sum(weights, axis=2)]
    dynamic_slice x96 -> x0, local copies, waits for them, and re-layouts: 65.7 us -> none  [the longest x32 37.7 us: body(): lax.scan(attend_block, start_state, (key_blocks, value_blocks, block_star...]
    reshape x3 -> x2, local copies, waits for them, and re-layouts: 64.4 us -> 2.91 us  [the longest x1 1.91 us: body(): by_place = m_all.reshape(slots, heads, row_tiles, 2, NZ, 2, row_tiles)]
  transfers between devices with their start and end apart: 4 -> 0, of which waited for: 3 -> 0; matrix products, arithmetic and copies ran while one was open for 57% -> 0% of each run, Pallas kernels for 0% -> 0%
where the time goes in v1:
time: 223 us
  Pallas kernels  217 us (97%)
  local copies, waits for them, and re-layouts  5.79 us (3%)
    pallas_call x1, Pallas kernels, spread(): pl.pallas_call(spread_kernel, out_shape=[jax.ShapeDtypeStruct((4, slab, w...  142 us
    pallas_call x1, Pallas kernels, attend(): pl.pallas_call(attend_kernel, out_shape=[jax.ShapeDtypeStruct((slots, wid...  39 us
    pallas_call x1, Pallas kernels, merge(): pl.pallas_call(merge_kernel, out_shape=jax.ShapeDtypeStruct((rows, w_all....  36 us

profile of v1, /device:TPU:1, one launch (start us, length us, event | category | flops | bytes accessed | tf_op | source)
XLA Modules:
  0.0 223.2 jit_solution(6769480361063795173)
XLA Ops:
  0.0 142.1 %spread.1 = (bf16[4,512,384]{2,1,0:T(8,128)(2,1)}, bf16[8,512,384]{2,1,0:T(8,128)(2,1)}, bf16[8,512,384]{2,1,0:T(8,128)(2,1)}, s32[4,3,4,128]{3,2,1,0:T(4,128)}, bf16[8,384,3072]{2,1,0:T(8,128)(2,1)}) custom-call(bf16[64,3072]{1,0:T(8,128)(2,1)} %q.1, bf16[64,3072]{1,0:T(8,128)(2,1)} %k.1, bf16[64,3072]{1,0:T(8,128)(2,1)} %v.1, s32[3,4,128]{2,1,0:T(4,128)} %m.1, ...), custom_call_target="tpu_custom_call" | custom-call | tf_op jit(solution)/shard_map/spread/pallas_call | solution.py:246
  142.1 1.9 reshape.28
  144.0 0.3 compare_select_fusion
  144.3 0.7 copy.8
  145.0 0.2 reshape.33
  145.1 0.3 broadcast_in_dim.13
  145.4 1.0 reshape.29.bias
  146.4 39.0 %attend.1 = (bf16[4,384,512]{2,1,0:T(8,128)(2,1)}, f32[4,8,512]{2,1,0:T(8,128)}) custom-call(f32[3,32,2048]{2,1,0:T(8,128)} %reshape.29.bias, bf16[2048,384]{1,0:T(8,128)(2,1)} %bitcast.10, bf16[4096,384]{1,0:T(8,128)(2,1)} %bitcast.8, bf16[4096,384]{1,0:T(8,128)(2,1)} %bitcast.9), custom_call_target="tpu_custom_call" | custom-call | tf_op jit(solution)/shard_map/attend/pallas_call | solution.py:338
  185.4 36.0 %merge.1 = bf16[64,3072]{1,0:T(8,128)(2,1)} custom-call(bf16[4,384,512]{2,1,0:T(8,128)(2,1)} %get-tuple-element.16.o, f32[4,8,512]{2,1,0:T(8,128)} %get-tuple-element.17.stat, bf16[8,384,3072]{2,1,0:T(8,128)(2,1)} %get-tuple-element.18.w), custom_call_target="tpu_custom_call" | custom-call | tf_op jit(solution)/shard_map/merge/pallas_call | solution.py:422
  221.4 1.8 copy.11

commit v2 on v1

v2 whole, which is shorter than its diff:
```python
import functools
import math

import jax
import jax.numpy as jnp
from jax import lax
from jax.experimental import pallas as pl
from jax.experimental.pallas import tpu as pltpu
from jax.sharding import PartitionSpec as P

HEAD_DIM = 128
TILE = 128
MESH = pl.DeviceIdType.MESH
TO_LOG2 = math.log2(math.e) / math.sqrt(HEAD_DIM)
LOW = -1e30
BLOCKED = 2e30
VMEM_LIMIT = 60 * 2**20
NX, NY, NZ = 2, 4, 8


def place():
    blk, head = lax.axis_index("blk"), lax.axis_index("head")
    return blk // 16, (blk // 2) % NZ, blk % 2, head // NY, head % NY


def at(x_hi, z, core, x_lo, y):
    return (x_hi * 16 + z * 2 + core, x_lo * NY + y)


def greet(peers):
    barrier = pltpu.get_barrier_semaphore()
    for peer in peers:
        pl.semaphore_signal(barrier, inc=1, device_id=peer, device_id_type=MESH)
    pl.semaphore_wait(barrier, len(peers))


class Wires:
    def __init__(self, send_sems, recv_sems, local_sems):
        self.send_sems, self.recv_sems, self.local_sems = send_sems, recv_sems, local_sems
        self.used, self.used_local = 0, 0
        self.sent = []

    def push(self, src, dst, peer, land=None):
        copy = pltpu.make_async_remote_copy(
            src_ref=src,
            dst_ref=dst,
            send_sem=self.send_sems.at[self.used],
            recv_sem=self.recv_sems.at[self.used],
            device_id=peer,
            device_id_type=MESH,
        )
        arrival = copy
        if land is not None:
            arrival = pltpu.make_async_remote_copy(
                src_ref=land,
                dst_ref=land,
                send_sem=self.send_sems.at[self.used],
                recv_sem=self.recv_sems.at[self.used],
                device_id=peer,
                device_id_type=MESH,
            )
        self.used += 1
        copy.start()
        self.sent.append(copy)
        return arrival

    def local(self, src, dst):
        copy = pltpu.make_async_copy(src, dst, self.local_sems.at[self.used_local])
        self.used_local += 1
        copy.start()
        return copy

    def finish(self):
        for copy in self.sent:
            copy.wait_send()


def fused_kernel(
    q, k, v, m, w,
    out, q_all, k_all, v_all, w_all,
    q_here, k_here, v_here, w_here, m_in, bias, query, acc, top_at, total_at,
    o, stat, o_in, stat_in, ready, mixed_in,
    send_sems, recv_sems, local_sems,
):
    x_hi, z, core, x_lo, y = place()
    rows = q.shape[0]
    heads, q_count = query.shape[0], query.shape[1]
    slots, slab, width = q_here.shape
    row_tiles = slab // TILE
    group = x_lo * NY + y
    other_hi, other_core, other_lo = 1 - x_hi, 1 - core, 1 - x_lo
    slot = x_hi * 2 + core
    sibling = at(x_hi, z, other_core, x_lo, y)
    across = at(other_hi, z, core, x_lo, y)
    diagonal = at(other_hi, z, other_core, x_lo, y)
    z_up, z_down = (z + 1) % NZ, (z + NZ - 1) % NZ
    up, down = at(x_hi, z_up, core, x_lo, y), at(x_hi, z_down, core, x_lo, y)
    y_up, y_down, y_far = (y + 1) % NY, (y + NY - 1) % NY, (y + 2) % NY
    partner = at(x_hi, z, core, other_lo, y)
    outer = at(other_hi, z, core, other_lo, y)
    blk = x_hi * 16 + z * 2 + core
    head_peers = [(group + step) % 8 for step in range(1, 8)]
    greet([(blk, peer) for peer in head_peers] + [sibling, across, diagonal, up, down, outer])
    wires = Wires(send_sems, recv_sems, local_sems)

    def exchange(src, dst):
        arrivals = []
        for step in range(1, 8):
            peer = (group + step) % 8
            origin = (group + 8 - step) % 8
            arrivals.append(
                wires.push(
                    src.at[:, pl.ds(pl.multiple_of(peer * width, 128), width)],
                    dst.at[pl.ds(pl.multiple_of(group * rows, 64), rows), :],
                    (blk, peer),
                    dst.at[pl.ds(pl.multiple_of(origin * rows, 64), rows), :],
                )
            )
        own = wires.local(
            src.at[:, pl.ds(pl.multiple_of(group * width, 128), width)],
            dst.at[pl.ds(pl.multiple_of(group * rows, 64), rows), :],
        )
        return arrivals, own

    def settle(pending):
        for arrival in pending[0]:
            arrival.wait_recv()
        pending[1].wait()

    k_wait = exchange(k, k_all.at[z])
    v_wait = exchange(v, v_all.at[z])
    q_wait = exchange(q, q_all.at[slot])
    m_wait = [
        wires.push(m, m_in.at[slot], sibling, m_in.at[x_hi * 2 + other_core]),
        wires.push(m, m_in.at[slot], across, m_in.at[other_hi * 2 + core]),
        wires.push(m, m_in.at[slot], diagonal, m_in.at[other_hi * 2 + other_core]),
    ]
    m_own = wires.local(m, m_in.at[slot])

    ring, loads = {}, {}

    def ring_step(full, step, direction):
        if direction > 0:
            held = (z + NZ - step) % NZ
            landing = (z + NZ - step - 1) % NZ
            return wires.push(full.at[held], full.at[held], up, full.at[landing]), landing
        held = (z + step) % NZ
        landing = (z + step + 1) % NZ
        return wires.push(full.at[held], full.at[held], down, full.at[landing]), landing

    def load(name, index):
        if name == "k":
            return wires.local(k_all.at[index], k_here.at[index])
        return wires.local(v_all.at[index], v_here.at[index])

    def ring_turn(step):
        loading = []
        for name, full in (("k", k_all), ("v", v_all)):
            for direction in (1, -1):
                key = (name, direction)
                if key not in ring:
                    continue
                arrival, index = ring[key]
                arrival.wait_recv()
                if step < (4 if key in (("k", 1), ("v", -1)) else 3):
                    ring[key] = ring_step(full, step, direction)
                else:
                    del ring[key]
                loading.append(load(name, index))
        return loading

    settle(k_wait)
    ring[("k", 1)] = ring_step(k_all, 0, 1)
    ring[("k", -1)] = ring_step(k_all, 0, -1)
    settle(v_wait)
    ring[("v", 1)] = ring_step(v_all, 0, 1)
    ring[("v", -1)] = ring_step(v_all, 0, -1)
    own_loads = [load("k", z), load("v", z)]

    depth = w.shape[0]
    half = depth // 2
    columns = w.shape[1] // 2
    mine = pl.ds(pl.multiple_of(core * columns, 128), columns)
    theirs = pl.ds(pl.multiple_of(other_core * columns, 128), columns)
    upper, lower, whole = pl.ds(0, half), pl.ds(half, half), pl.ds(0, depth)

    def w_part(lo, yy, part, cols=mine):
        return w_all.at[lo * NY + yy, part, cols]

    def w_cross(source, yy):
        return (
            wires.push(source(upper), w_part(x_lo, yy, upper), partner, w_part(other_lo, yy, upper)),
            wires.push(source(lower), w_part(x_lo, yy, lower), outer, w_part(other_lo, yy, lower)),
        )

    swaps = []

    def w_swap(lo, yy, part):
        swaps.append(
            wires.push(w_part(lo, yy, part), w_part(lo, yy, part), sibling, w_part(lo, yy, part, theirs))
        )

    settle(q_wait)
    q_side = wires.push(q_all.at[slot], q_all.at[slot], sibling, q_all.at[x_hi * 2 + other_core])
    q_across = wires.push(q_all.at[slot], q_all.at[slot], across, q_all.at[other_hi * 2 + core])
    w_up = wires.push(w.at[:, mine], w_part(x_lo, y, whole), (blk, x_lo * NY + y_up), w_part(x_lo, y_down, whole))
    w_down = wires.push(w.at[:, mine], w_part(x_lo, y, whole), (blk, x_lo * NY + y_down), w_part(x_lo, y_up, whole))
    crossing = [w_cross(lambda part: w.at[part, mine], y)]

    acc[...] = jnp.zeros_like(acc)
    stat[...] = jnp.zeros_like(stat)
    top_at[...] = jnp.full_like(top_at, LOW)
    total_at[...] = jnp.zeros_like(total_at)
    for arrival in m_wait:
        arrival.wait_recv()
    m_own.wait()
    tile_rows = slots * row_tiles
    spread_rows = lax.broadcasted_iota(jnp.int32, (tile_rows, q_count), 0)
    spread_cols = lax.broadcasted_iota(jnp.int32, (tile_rows, q_count), 1)
    spread = jnp.where(spread_cols // TILE == spread_rows, 1.0, 0.0).astype(jnp.bfloat16)
    for head in range(heads):
        allowed = jnp.concatenate([m_in[s, head] for s in range(slots)], axis=0)
        allowed = jnp.where(allowed > 0, 1.0, 0.0).astype(jnp.bfloat16)
        wide = lax.dot_general(allowed, spread, (((0,), (0,)), ((), ())), preferred_element_type=jnp.float32)
        bias[head] = (1.0 - wide) * BLOCKED

    q_across.wait_recv()
    q_diagonal = wires.push(
        q_all.at[other_hi * 2 + core],
        q_all.at[other_hi * 2 + core],
        sibling,
        q_all.at[other_hi * 2 + other_core],
    )
    q_side.wait_recv()
    first_turn = ring_turn(1)
    q_diagonal.wait_recv()
    q_load = wires.local(q_all, q_here)
    q_load.wait()
    for head in range(heads):
        for s in range(slots):
            scaled = q_here[s, :, head * HEAD_DIM : (head + 1) * HEAD_DIM].astype(jnp.float32) * TO_LOG2
            coarse = scaled.astype(jnp.bfloat16)
            at_rows = slice(s * slab, (s + 1) * slab)
            query[head, at_rows, :HEAD_DIM] = coarse
            query[head, at_rows, HEAD_DIM:] = (scaled - coarse.astype(jnp.float32)).astype(jnp.bfloat16)

    ones = jnp.ones((16, slab), jnp.bfloat16)

    def work(loading, first, second=None):
        for one in loading:
            one.wait()

        def one_head(i, unused):
            head, turn = i % heads, i // heads
            index = first if second is None else first + turn * (second - first)
            lanes = pl.ds(pl.multiple_of(head * HEAD_DIM, HEAD_DIM), HEAD_DIM)
            key = k_here[index, :, lanes]
            scores = lax.dot_general(
                jnp.concatenate([key, key], axis=1),
                query[head],
                (((1,), (1,)), ((), ())),
                preferred_element_type=jnp.float32,
            )
            first_tile = (x_hi * 2 * NZ + index * 2 + core) * row_tiles
            blocked = [bias[head, pl.ds(first_tile + a, 1), :] for a in range(row_tiles)]
            top = top_at[head]
            next_top = top
            for a in range(row_tiles):
                tile_top = jnp.max(scores[a * TILE : (a + 1) * TILE], axis=0, keepdims=True)
                next_top = jnp.maximum(next_top, tile_top - blocked[a])
            weights = jnp.concatenate(
                [
                    jnp.exp2(scores[a * TILE : (a + 1) * TILE] - (next_top + blocked[a])).astype(jnp.bfloat16)
                    for a in range(row_tiles)
                ],
                axis=0,
            )
            shrink = jnp.exp2(top - next_top)
            added = lax.dot_general(
                jnp.concatenate([v_here[index, :, lanes].T, ones], axis=0),
                weights,
                (((1,), (0,)), ((), ())),
                preferred_element_type=jnp.float32,
            )
            acc[head] = acc[head] * shrink + added[:HEAD_DIM]
            top_at[head] = next_top
            total_at[head] = total_at[head] * shrink + added[HEAD_DIM : HEAD_DIM + 1]
            return unused

        lax.fori_loop(0, heads if second is None else 2 * heads, one_head, 0)

    def crossed(index, yy):
        crossing[index][0].wait_recv()
        w_swap(other_lo, yy, upper)
        crossing[index][1].wait_recv()
        w_swap(other_lo, yy, lower)

    work(own_loads, z)
    work(first_turn, z_down, z_up)
    w_up.wait_recv()
    far_up = wires.push(
        w_part(x_lo, y_down, upper), w_part(x_lo, y_down, upper), (blk, x_lo * NY + y_up), w_part(x_lo, y_far, upper)
    )
    w_down.wait_recv()
    far_down = wires.push(
        w_part(x_lo, y_up, lower), w_part(x_lo, y_up, lower), (blk, x_lo * NY + y_down), w_part(x_lo, y_far, lower)
    )
    crossing.append(w_cross(functools.partial(w_part, x_lo, y_down), y_down))
    crossing.append(w_cross(functools.partial(w_part, x_lo, y_up), y_up))
    w_swap(x_lo, y_down, whole)
    w_swap(x_lo, y_up, whole)
    crossed(0, y)
    turn = ring_turn(2)
    work(turn, (z + NZ - 2) % NZ, (z + 2) % NZ)
    far_up.wait_recv()
    far_down.wait_recv()
    crossing.append(w_cross(functools.partial(w_part, x_lo, y_far), y_far))
    w_swap(x_lo, y_far, whole)
    turn = ring_turn(3)
    crossed(1, y_down)
    crossed(2, y_up)
    work(turn, (z + NZ - 3) % NZ, (z + 3) % NZ)
    turn = ring_turn(4)
    work(turn, (z + 4) % NZ)
    crossed(3, y_far)

    for head in range(heads):
        mean = (acc[head] / jnp.maximum(total_at[head], 1e-30)).astype(jnp.bfloat16)
        for s in range(slots):
            cols = slice(s * slab, (s + 1) * slab)
            o[s, head * HEAD_DIM : (head + 1) * HEAD_DIM, :] = mean[:, cols]
            stat[s, head : head + 1, :] = top_at[head, :, cols]
            stat[s, heads + head : heads + head + 1, :] = total_at[head, :, cols]
    arrivals = []
    for hi, c, peer in ((other_hi, core, across), (other_hi, other_core, diagonal), (x_hi, other_core, sibling)):
        peer_slot = hi * 2 + c
        arrivals.append(wires.push(o.at[peer_slot], o_in.at[slot], peer, o_in.at[peer_slot]))
        arrivals.append(wires.push(stat.at[peer_slot], stat_in.at[slot], peer, stat_in.at[peer_slot]))
    o_in[slot] = o[slot]
    stat_in[slot] = stat[slot]
    for arrival in swaps:
        arrival.wait_recv()
    w_loads = [wires.local(w, w_here.at[group])] + [wires.local(w_all.at[g], w_here.at[g]) for g in head_peers]
    for arrival in arrivals:
        arrival.wait_recv()
    for head in range(heads):
        tops = [stat_in[s, head : head + 1, :] for s in range(slots)]
        best = functools.reduce(jnp.maximum, tops)
        shares = [stat_in[s, heads + head : heads + head + 1, :] * jnp.exp2(tops[s] - best) for s in range(slots)]
        total = functools.reduce(jnp.add, shares)
        band = slice(head * HEAD_DIM, (head + 1) * HEAD_DIM)
        blend = functools.reduce(
            jnp.add,
            [o_in[s, band, :].astype(jnp.float32) * (shares[s] / total) for s in range(slots)],
        )
        ready[:, band] = blend.T.astype(jnp.bfloat16)
    pieces = []
    for step in range(1, 8):
        peer = (group + step) % 8
        origin = (group + 8 - step) % 8
        pieces.append(
            wires.push(
                ready.at[pl.ds(pl.multiple_of(peer * rows, 64), rows), :],
                mixed_in.at[group],
                (blk, peer),
                mixed_in.at[origin],
            )
        )
    mixed_in[group] = ready[pl.ds(pl.multiple_of(group * rows, 64), rows), :]
    for one in w_loads:
        one.wait()
    for piece in pieces:
        piece.wait_recv()
    cols = 768
    for c in range(out.shape[1] // cols):
        mixed = jnp.zeros((rows, cols), jnp.float32)
        for g in range(8):
            mixed += jnp.dot(
                mixed_in[g], w_here[g, :, c * cols : (c + 1) * cols], preferred_element_type=jnp.float32
            )
        out[:, c * cols : (c + 1) * cols] = mixed.astype(jnp.bfloat16)
    wires.finish()


def body(queries, keys, values, tile_mask, out_weight):
    rows = queries.shape[0]
    width = queries.shape[1] // 8
    heads = width // HEAD_DIM
    slab, slots = rows * 8, 4
    q_count = slots * slab
    bf16, f32 = jnp.bfloat16, jnp.float32
    hbm = pl.BlockSpec(memory_space=pl.ANY)
    w_shape = (8,) + out_weight.shape
    return pl.pallas_call(
        fused_kernel,
        out_shape=[
            jax.ShapeDtypeStruct(queries.shape, bf16),
            jax.ShapeDtypeStruct((slots, slab, width), bf16),
            jax.ShapeDtypeStruct((NZ, slab, width), bf16),
            jax.ShapeDtypeStruct((NZ, slab, width), bf16),
            jax.ShapeDtypeStruct(w_shape, bf16),
        ],
        in_specs=[hbm] * 5,
        out_specs=[pl.BlockSpec(memory_space=pltpu.VMEM)] + [hbm] * 4,
        scratch_shapes=[
            pltpu.VMEM((slots, slab, width), bf16),
            pltpu.VMEM((NZ, slab, width), bf16),
            pltpu.VMEM((NZ, slab, width), bf16),
            pltpu.VMEM(w_shape, bf16),
            pltpu.VMEM((slots,) + tile_mask.shape, jnp.int32),
            pltpu.VMEM((heads, tile_mask.shape[2], q_count), f32),
            pltpu.VMEM((heads, q_count, 2 * HEAD_DIM), bf16),
            pltpu.VMEM((heads, HEAD_DIM, q_count), f32),
            pltpu.VMEM((heads, 1, q_count), f32),
            pltpu.VMEM((heads, 1, q_count), f32),
            pltpu.VMEM((slots, width, slab), bf16),
            pltpu.VMEM((slots, 8, slab), f32),
            pltpu.VMEM((slots, width, slab), bf16),
            pltpu.VMEM((slots, 8, slab), f32),
            pltpu.VMEM((slab, width), bf16),
            pltpu.VMEM((8, rows, width), bf16),
            pltpu.SemaphoreType.DMA((80,)),
            pltpu.SemaphoreType.DMA((80,)),
            pltpu.SemaphoreType.DMA((40,)),
        ],
        name="fused",
        compiler_params=pltpu.CompilerParams(
            collective_id=1, has_side_effects=True, vmem_limit_bytes=VMEM_LIMIT
        ),
    )(queries, keys, values, tile_mask, out_weight)[0]


def solution(mesh):
    placed = (
        P(("blk", "head"), None),
        P(("blk", "head"), None),
        P(("blk", "head"), None),
        P("head", "blk", None),
        P("head", None),
    )
    return jax.shard_map(
        body, mesh=mesh, in_specs=placed, out_specs=P(("blk", "head"), None), check_vma=False
    )
```

time: 223 us -> 128 us (0.57)
  Pallas kernels: 217 us -> 125 us
  local copies, waits for them, and re-layouts: 5.79 us -> 1.77 us
    pallas_call x3 -> x1, Pallas kernels: 217 us -> 125 us  [body(): pl.pallas_call(fused_kernel, out_shape=[jax.ShapeDtypeStruct(queries.shap...]
    reshape x2 -> x0, local copies, waits for them, and re-layouts: 2.91 us -> none  [the longest x1 1.91 us: body(): by_place = m_all.reshape(slots, heads, row_tiles, 2, NZ, 2, row_tiles)]
where the time goes in v2:
time: 128 us; the launch traced here: 127 us
  Pallas kernels  125 us (98%)
  local copies, waits for them, and re-layouts  1.77 us (1%)
    pallas_call x1, Pallas kernels, body(): pl.pallas_call(fused_kernel, out_shape=[jax.ShapeDtypeStruct(queries.shap...  125 us

profile of v2, /device:TPU:1, one launch (start us, length us, event | category | flops | bytes accessed | tf_op | source)
XLA Modules:
  0.0 126.9 jit_solution(11080645929085975832)
XLA Ops:
  0.0 125.2 %fused.1 = (bf16[64,3072]{1,0:T(8,128)(2,1)}, bf16[4,512,384]{2,1,0:T(8,128)(2,1)}, bf16[8,512,384]{2,1,0:T(8,128)(2,1)}, bf16[8,512,384]{2,1,0:T(8,128)(2,1)}, bf16[8,384,3072]{2,1,0:T(8,128)(2,1)}) custom-call(bf16[64,3072]{1,0:T(8,128)(2,1)} %q.1, bf16[64,3072]{1,0:T(8,128)(2,1)} %k.1, bf16[64,3072]{1,0:T(8,128)(2,1)} %v.1, s32[3,4,128]{2,1,0:T(4,128)} %m.1, ...), custom_call_target="tpu_custom_call" | custom-call | tf_op jit(solution)/shard_map/fused/pallas_call | solution.py:394
  125.2 1.8 %copy.7 = bf16[64,3072]{1,0:T(8,128)(2,1)} copy(bf16[64,3072]{1,0:T(8,128)(2,1)} %get-tuple-element.6) | data formatting | bytes 786432

commit v3 on v2

v3 whole, which is shorter than its diff:
```python
import functools
import math

import jax
import jax.numpy as jnp
from jax import lax
from jax.experimental import pallas as pl
from jax.experimental.pallas import tpu as pltpu
from jax.sharding import PartitionSpec as P

HEAD_DIM = 128
TILE = 128
MESH = pl.DeviceIdType.MESH
TO_LOG2 = math.log2(math.e) / math.sqrt(HEAD_DIM)
LOW = -1e30
BLOCKED = 2e30
VMEM_LIMIT = 60 * 2**20
NX, NY, NZ = 2, 4, 8


def place():
    blk, head = lax.axis_index("blk"), lax.axis_index("head")
    return blk // 16, (blk // 2) % NZ, blk % 2, head // NY, head % NY


def at(x_hi, z, core, x_lo, y):
    return (x_hi * 16 + z * 2 + core, x_lo * NY + y)


def greet(peers):
    barrier = pltpu.get_barrier_semaphore()
    for peer in peers:
        pl.semaphore_signal(barrier, inc=1, device_id=peer, device_id_type=MESH)
    pl.semaphore_wait(barrier, len(peers))


class Wires:
    def __init__(self, send_sems, recv_sems, local_sems):
        self.send_sems, self.recv_sems, self.local_sems = send_sems, recv_sems, local_sems
        self.used, self.used_local = 0, 0
        self.sent = []

    def push(self, src, dst, peer, land=None):
        copy = pltpu.make_async_remote_copy(
            src_ref=src,
            dst_ref=dst,
            send_sem=self.send_sems.at[self.used],
            recv_sem=self.recv_sems.at[self.used],
            device_id=peer,
            device_id_type=MESH,
        )
        arrival = copy
        if land is not None:
            arrival = pltpu.make_async_remote_copy(
                src_ref=land,
                dst_ref=land,
                send_sem=self.send_sems.at[self.used],
                recv_sem=self.recv_sems.at[self.used],
                device_id=peer,
                device_id_type=MESH,
            )
        self.used += 1
        copy.start()
        self.sent.append(copy)
        return arrival

    def local(self, src, dst):
        copy = pltpu.make_async_copy(src, dst, self.local_sems.at[self.used_local])
        self.used_local += 1
        copy.start()
        return copy

    def finish(self):
        for copy in self.sent:
            copy.wait_send()


def fused_kernel(
    q, k, v, m, w,
    out, k_all, v_all, w_all,
    q_here, k_here, v_here, w_here, m_in, bias, query, acc, top_at, total_at,
    o, stat, o_in, stat_in, ready, mixed_in, mixed, result,
    send_sems, recv_sems, local_sems,
):
    x_hi, z, core, x_lo, y = place()
    rows = q.shape[0]
    heads, slots, slab = q_here.shape[0], q_here.shape[1], q_here.shape[2]
    width = heads * HEAD_DIM
    row_tiles = slab // TILE
    q_count = slots * slab
    group = x_lo * NY + y
    other_hi, other_core, other_lo = 1 - x_hi, 1 - core, 1 - x_lo
    slot = x_hi * 2 + core
    sibling_slot, across_slot, diagonal_slot = x_hi * 2 + other_core, other_hi * 2 + core, other_hi * 2 + other_core
    sibling = at(x_hi, z, other_core, x_lo, y)
    across = at(other_hi, z, core, x_lo, y)
    diagonal = at(other_hi, z, other_core, x_lo, y)
    z_up, z_down = (z + 1) % NZ, (z + NZ - 1) % NZ
    up, down = at(x_hi, z_up, core, x_lo, y), at(x_hi, z_down, core, x_lo, y)
    y_up, y_down, y_far = (y + 1) % NY, (y + NY - 1) % NY, (y + 2) % NY
    partner = at(x_hi, z, core, other_lo, y)
    outer = at(other_hi, z, core, other_lo, y)
    blk = x_hi * 16 + z * 2 + core
    head_peers = [(group + step) % 8 for step in range(1, 8)]
    neighbour = at(x_hi, z, other_core, x_lo, y + 1 - 2 * (y % 2))
    greet([(blk, peer) for peer in head_peers] + [sibling, across, diagonal, up, down, outer, neighbour])
    wires = Wires(send_sems, recv_sems, local_sems)
    my_rows = pl.ds(pl.multiple_of(group * rows, 64), rows)

    def feature(owner, head):
        return pl.ds(pl.multiple_of(owner * width + head * HEAD_DIM, HEAD_DIM), HEAD_DIM)

    def exchange(src, dst, head):
        arrivals = []
        for step in range(1, 8):
            peer = (group + step) % 8
            origin = (group + 8 - step) % 8
            arrivals.append(
                wires.push(
                    src.at[:, feature(peer, head)],
                    dst.at[my_rows, :],
                    (blk, peer),
                    dst.at[pl.ds(pl.multiple_of(origin * rows, 64), rows), :],
                )
            )
        return arrivals, wires.local(src.at[:, feature(group, head)], dst.at[my_rows, :])

    def settle(pending):
        for arrival in pending[0]:
            arrival.wait_recv()
        pending[1].wait()

    waits = {}

    def exchange_head(head):
        waits["k", head] = exchange(k, k_all.at[head, z], head)
        waits["v", head] = exchange(v, v_all.at[head, z], head)
        waits["q", head] = exchange(q, q_here.at[head, slot], head)

    ring = {}

    def ring_step(full, head, step, direction):
        if direction > 0:
            held, landing, peer = (z + NZ - step) % NZ, (z + NZ - step - 1) % NZ, up
        else:
            held, landing, peer = (z + step) % NZ, (z + step + 1) % NZ, down
        here = full.at[head, held]
        return wires.push(here, here, peer, full.at[head, landing]), landing

    def load(name, head, index):
        if name == "k":
            return wires.local(k_all.at[head, index], k_here.at[head, index])
        return wires.local(v_all.at[head, index], v_here.at[head, index])

    def ring_start(head):
        loading = []
        for name, full in (("k", k_all), ("v", v_all)):
            settle(waits[name, head])
            for direction in (1, -1):
                ring[head, name, direction] = ring_step(full, head, 0, direction)
            loading.append(load(name, head, z))
        return loading

    def ring_turn(head, step):
        loading = []
        for name, full in (("k", k_all), ("v", v_all)):
            for direction in (1, -1):
                last = 4 if (name, direction) in (("k", 1), ("v", -1)) else 3
                if step > last:
                    continue
                arrival, index = ring[head, name, direction]
                arrival.wait_recv()
                if step < last:
                    ring[head, name, direction] = ring_step(full, head, step, direction)
                loading.append(load(name, head, index))
        return loading

    moving = {}

    def queries_out(head):
        settle(waits["q", head])
        mine = q_here.at[head, slot]
        moving["side", head] = wires.push(mine, mine, sibling, q_here.at[head, sibling_slot])
        moving["across", head] = wires.push(mine, mine, across, q_here.at[head, across_slot])

    def queries_on(head):
        moving["across", head].wait_recv()
        theirs = q_here.at[head, across_slot]
        moving["diagonal", head] = wires.push(theirs, theirs, sibling, q_here.at[head, diagonal_slot])

    def queries_in(head):
        moving["side", head].wait_recv()
        moving["diagonal", head].wait_recv()
        for s in range(slots):
            scaled = q_here[head, s].astype(jnp.float32) * TO_LOG2
            coarse = scaled.astype(jnp.bfloat16)
            at_rows = slice(s * slab, (s + 1) * slab)
            query[head, at_rows, :HEAD_DIM] = coarse
            query[head, at_rows, HEAD_DIM:] = (scaled - coarse.astype(jnp.float32)).astype(jnp.bfloat16)

    depth = w.shape[0]
    half = depth // 2
    quarter = w.shape[1] // 4
    parity = y % 2
    y_pair = y + 1 - 2 * parity
    beside = at(x_hi, z, core, x_lo, y_pair)
    mine = pl.ds(pl.multiple_of((parity * 2 + core) * quarter, 128), quarter)
    next_door = pl.ds(pl.multiple_of(((1 - parity) * 2 + core) * quarter, 128), quarter)
    upper, lower = pl.ds(0, half), pl.ds(half, half)

    def w_along(peer_y, from_y, cols):
        return wires.push(w.at[:, cols], w_all.at[group], (blk, x_lo * NY + peer_y), w_all.at[x_lo * NY + from_y])

    def w_cross(yy, own=False):
        arrivals = []
        for part, peer in ((upper, partner), (lower, outer)):
            held = w.at[part, mine] if own else w_all.at[x_lo * NY + yy, part]
            arrivals.append(
                wires.push(held, w_all.at[x_lo * NY + yy, part], peer, w_all.at[other_lo * NY + yy, part])
            )
        return arrivals

    def make_bias(head):
        tile_rows = slots * row_tiles
        spread_rows = lax.broadcasted_iota(jnp.int32, (tile_rows, q_count), 0)
        spread_cols = lax.broadcasted_iota(jnp.int32, (tile_rows, q_count), 1)
        spread = jnp.where(spread_cols // TILE == spread_rows, 1.0, 0.0).astype(jnp.bfloat16)
        allowed = jnp.concatenate([m_in[s, head] for s in range(slots)], axis=0)
        allowed = jnp.where(allowed > 0, 1.0, 0.0).astype(jnp.bfloat16)
        wide = lax.dot_general(allowed, spread, (((0,), (0,)), ((), ())), preferred_element_type=jnp.float32)
        bias[head] = (1.0 - wide) * BLOCKED

    ones = jnp.ones((16, slab), jnp.bfloat16)

    def work(head, loading, first, second=None):
        for one in loading:
            one.wait()

        def one_block(i, unused):
            index = first if second is None else first + i * (second - first)
            key = k_here[head, index]
            scores = lax.dot_general(
                jnp.concatenate([key, key], axis=1),
                query[head],
                (((1,), (1,)), ((), ())),
                preferred_element_type=jnp.float32,
            )
            first_tile = (x_hi * 2 * NZ + index * 2 + core) * row_tiles
            blocked = [bias[head, pl.ds(first_tile + a, 1), :] for a in range(row_tiles)]
            top = top_at[head]
            next_top = top
            for a in range(row_tiles):
                tile_top = jnp.max(scores[a * TILE : (a + 1) * TILE], axis=0, keepdims=True)
                next_top = jnp.maximum(next_top, tile_top - blocked[a])
            weights = jnp.concatenate(
                [
                    jnp.exp2(scores[a * TILE : (a + 1) * TILE] - (next_top + blocked[a])).astype(jnp.bfloat16)
                    for a in range(row_tiles)
                ],
                axis=0,
            )
            shrink = jnp.exp2(top - next_top)
            added = lax.dot_general(
                jnp.concatenate([v_here[head, index].T, ones], axis=0),
                weights,
                (((1,), (0,)), ((), ())),
                preferred_element_type=jnp.float32,
            )
            acc[head] = acc[head] * shrink + added[:HEAD_DIM]
            top_at[head] = next_top
            total_at[head] = total_at[head] * shrink + added[HEAD_DIM : HEAD_DIM + 1]
            return unused

        lax.fori_loop(0, 1 if second is None else 2, one_block, 0)

    def partial_out(head):
        mean = (acc[head] / jnp.maximum(total_at[head], 1e-30)).astype(jnp.bfloat16)
        for s in range(slots):
            cols = slice(s * slab, (s + 1) * slab)
            o[head, s] = mean[:, cols]
            stat[head, s, 0:1, :] = top_at[head, :, cols]
            stat[head, s, 1:2, :] = total_at[head, :, cols]
        arrivals = []
        for peer_slot, peer in ((across_slot, across), (diagonal_slot, diagonal), (sibling_slot, sibling)):
            arrivals.append(wires.push(o.at[head, peer_slot], o_in.at[head, slot], peer, o_in.at[head, peer_slot]))
            arrivals.append(
                wires.push(stat.at[head, peer_slot], stat_in.at[head, slot], peer, stat_in.at[head, peer_slot])
            )
        o_in[head, slot] = o[head, slot]
        stat_in[head, slot] = stat[head, slot]
        return arrivals

    def partial_in(head, arrivals):
        for arrival in arrivals:
            arrival.wait_recv()
        tops = [stat_in[head, s, 0:1, :] for s in range(slots)]
        best = functools.reduce(jnp.maximum, tops)
        shares = [stat_in[head, s, 1:2, :] * jnp.exp2(tops[s] - best) for s in range(slots)]
        total = functools.reduce(jnp.add, shares)
        blend = functools.reduce(
            jnp.add, [o_in[head, s].astype(jnp.float32) * (shares[s] / total) for s in range(slots)]
        )
        ready[head] = blend.T.astype(jnp.bfloat16)
        my_lanes = pl.ds(pl.multiple_of(group * HEAD_DIM, HEAD_DIM), HEAD_DIM)
        pieces = []
        for step in range(1, 8):
            peer = (group + step) % 8
            origin = (group + 8 - step) % 8
            pieces.append(
                wires.push(
                    ready.at[head, pl.ds(pl.multiple_of(peer // 2 * 2 * rows, 128), 2 * rows), :],
                    mixed_in.at[head, core, :, my_lanes],
                    (blk, peer),
                    mixed_in.at[head, core, :, pl.ds(pl.multiple_of(origin * HEAD_DIM, HEAD_DIM), HEAD_DIM)],
                )
            )
        mixed_in[head, core, :, my_lanes] = ready[head, pl.ds(pl.multiple_of(group // 2 * 2 * rows, 128), 2 * rows), :]
        return pieces

    def share(head, pieces):
        for piece in pieces:
            piece.wait_recv()
        held = mixed_in.at[head, core]
        return wires.push(held, held, sibling, mixed_in.at[head, other_core])

    def project(head, shared):
        shared.wait_recv()
        tokens = mixed_in[head].reshape(4 * rows, 8 * HEAD_DIM)
        part = jnp.dot(tokens, w_here[head], preferred_element_type=jnp.float32)
        if head == 0:
            mixed[...] = part
        elif head < heads - 1:
            mixed[...] += part
        else:
            result[...] = (mixed[...] + part).astype(jnp.bfloat16)

    def pair(step):
        return (z + NZ - step) % NZ, (z + step) % NZ

    exchange_head(0)
    m_wait = [
        wires.push(m, m_in.at[slot], sibling, m_in.at[sibling_slot]),
        wires.push(m, m_in.at[slot], across, m_in.at[across_slot]),
        wires.push(m, m_in.at[slot], diagonal, m_in.at[diagonal_slot]),
    ]
    m_own = wires.local(m, m_in.at[slot])
    exchange_head(1)
    own = [ring_start(0)]
    queries_out(0)
    exchange_head(2)
    own.append(ring_start(1))
    queries_out(1)
    own.append(ring_start(2))
    queries_out(2)
    w_crossed = [w_cross(y, True)]
    w_near = [w_along(y_up, y_down, next_door), w_along(y_down, y_up, next_door)]
    w_far = w_along(y_far, y_far, mine)
    acc[...] = jnp.zeros_like(acc)
    stat[...] = jnp.zeros_like(stat)
    top_at[...] = jnp.full_like(top_at, LOW)
    total_at[...] = jnp.zeros_like(total_at)
    for arrival in m_wait:
        arrival.wait_recv()
    m_own.wait()
    for head in range(heads):
        make_bias(head)

    for head in range(heads):
        queries_on(head)
        turn = ring_turn(head, 1)
        queries_in(head)
        work(head, own[head], z)
        work(head, turn, *pair(1))
    for head in range(heads):
        work(head, ring_turn(head, 2), *pair(2))
    for arrival in w_near:
        arrival.wait_recv()
    w_crossed += [w_cross(y_down), w_cross(y_up)]
    w_far.wait_recv()
    w_crossed.append(w_cross(y_far))
    for head in range(heads):
        work(head, ring_turn(head, 3), *pair(3))
    partial = []
    for head in range(heads - 1):
        work(head, ring_turn(head, 4), (z + 4) % NZ)
        partial.append(partial_out(head))
    turn = ring_turn(heads - 1, 4)
    for arrivals in w_crossed:
        for arrival in arrivals:
            arrival.wait_recv()
    w_loads = []
    for head in range(heads):
        band = pl.ds(head * HEAD_DIM, HEAD_DIM)
        for owner, source in [(group, w.at[:, mine])] + [(g, w_all.at[g]) for g in head_peers]:
            to_band = pl.ds(pl.multiple_of(owner * HEAD_DIM, HEAD_DIM), HEAD_DIM)
            w_loads.append(wires.local(source.at[band, :], w_here.at[head, to_band, :]))
    pieces = [partial_in(0, partial[0])]
    work(heads - 1, turn, (z + 4) % NZ)
    partial.append(partial_out(heads - 1))
    pieces.append(partial_in(1, partial[1]))
    shared = [share(0, pieces[0])]
    pieces.append(partial_in(2, partial[2]))
    shared.append(share(1, pieces[1]))
    for one in w_loads:
        one.wait()
    project(0, shared[0])
    project(1, shared[1])
    shared.append(share(2, pieces[2]))
    project(2, shared[2])

    def result_rows(c, odd):
        return pl.ds(pl.multiple_of((c * 2 + odd) * rows, 64), rows)

    from_core = pl.ds(pl.multiple_of((parity * 2 + other_core) * quarter, 128), quarter)
    from_beside = pl.ds(pl.multiple_of(((1 - parity) * 2 + core) * quarter, 128), quarter)
    from_opposite = pl.ds(pl.multiple_of(((1 - parity) * 2 + other_core) * quarter, 128), quarter)
    returns = [
        wires.push(result.at[result_rows(core, 1 - parity), :], out.at[:, mine], beside, out.at[:, from_beside]),
        wires.push(result.at[result_rows(other_core, 1 - parity), :], out.at[:, mine], neighbour, out.at[:, from_opposite]),
        wires.push(result.at[result_rows(other_core, parity), :], out.at[:, mine], sibling, out.at[:, from_core]),
    ]
    out[:, mine] = result[result_rows(core, parity), :]
    for arrival in returns:
        arrival.wait_recv()
    wires.finish()


def body(queries, keys, values, tile_mask, out_weight):
    rows, features = queries.shape
    heads = tile_mask.shape[0]
    slab, slots = rows * 8, 4
    q_count = slots * slab
    bf16, f32 = jnp.bfloat16, jnp.float32
    hbm = pl.BlockSpec(memory_space=pl.ANY)
    quarter = out_weight.shape[1] // 4
    w_shape = (8, out_weight.shape[0], quarter)
    vmem = pltpu.VMEM
    return pl.pallas_call(
        fused_kernel,
        out_shape=[
            jax.ShapeDtypeStruct(queries.shape, bf16),
            jax.ShapeDtypeStruct((heads, NZ, slab, HEAD_DIM), bf16),
            jax.ShapeDtypeStruct((heads, NZ, slab, HEAD_DIM), bf16),
            jax.ShapeDtypeStruct(w_shape, bf16),
        ],
        in_specs=[hbm] * 5,
        out_specs=[pl.BlockSpec(memory_space=vmem)] + [hbm] * 3,
        scratch_shapes=[
            vmem((heads, slots, slab, HEAD_DIM), bf16),
            vmem((heads, NZ, slab, HEAD_DIM), bf16),
            vmem((heads, NZ, slab, HEAD_DIM), bf16),
            vmem((heads, 8 * HEAD_DIM, quarter), bf16),
            vmem((slots,) + tile_mask.shape, jnp.int32),
            vmem((heads, tile_mask.shape[2], q_count), f32),
            vmem((heads, q_count, 2 * HEAD_DIM), bf16),
            vmem((heads, HEAD_DIM, q_count), f32),
            vmem((heads, 1, q_count), f32),
            vmem((heads, 1, q_count), f32),
            vmem((heads, slots, HEAD_DIM, slab), bf16),
            vmem((heads, slots, 8, slab), f32),
            vmem((heads, slots, HEAD_DIM, slab), bf16),
            vmem((heads, slots, 8, slab), f32),
            vmem((heads, slab, HEAD_DIM), bf16),
            vmem((heads, 2, 2 * rows, 8 * HEAD_DIM), bf16),
            vmem((4 * rows, quarter), f32),
            vmem((4 * rows, quarter), bf16),
            pltpu.SemaphoreType.DMA((192,)),
            pltpu.SemaphoreType.DMA((192,)),
            pltpu.SemaphoreType.DMA((96,)),
        ],
        name="fused",
        compiler_params=pltpu.CompilerParams(
            collective_id=1, has_side_effects=True, vmem_limit_bytes=VMEM_LIMIT
        ),
    )(queries, keys, values, tile_mask, out_weight)[0]


def solution(mesh):
    placed = (
        P(("blk", "head"), None),
        P(("blk", "head"), None),
        P(("blk", "head"), None),
        P("head", "blk", None),
        P("head", None),
    )
    return jax.shard_map(
        body, mesh=mesh, in_specs=placed, out_specs=P(("blk", "head"), None), check_vma=False
    )
```

time: 128 us -> 120 us (0.938)
  Pallas kernels: 125 us -> 118 us
    pallas_call x1, Pallas kernels: 125 us -> 118 us  [body(): pl.pallas_call(fused_kernel, out_shape=[jax.ShapeDtypeStruct(queries.shap...]
where the time goes in v3:
time: 120 us
  Pallas kernels  118 us (98%)
  local copies, waits for them, and re-layouts  1.77 us (1%)
    pallas_call x1, Pallas kernels, body(): pl.pallas_call(fused_kernel, out_shape=[jax.ShapeDtypeStruct(queries.shap...  118 us

profile of v3, /device:TPU:1, one launch (start us, length us, event | category | flops | bytes accessed | tf_op | source)
XLA Modules:
  0.0 120.2 jit_solution(5311182739099390799)
XLA Ops:
  0.0 118.4 %fused.1 = (bf16[64,3072]{1,0:T(8,128)(2,1)}, bf16[3,8,512,128]{3,2,1,0:T(8,128)(2,1)}, bf16[3,8,512,128]{3,2,1,0:T(8,128)(2,1)}, bf16[8,384,768]{2,1,0:T(8,128)(2,1)}) custom-call(bf16[64,3072]{1,0:T(8,128)(2,1)} %q.1, bf16[64,3072]{1,0:T(8,128)(2,1)} %k.1, bf16[64,3072]{1,0:T(8,128)(2,1)} %v.1, s32[3,4,128]{2,1,0:T(4,128)} %m.1, bf16[384,3072]{1,0:T(8,128)(2,1)} %w.1), custom_call_target="tpu_custom_call" | custom-call | tf_op jit(solution)/shard_map/fused/pallas_call | solution.py:438
  118.4 1.8 %copy.7 = bf16[64,3072]{1,0:T(8,128)(2,1)} copy(bf16[64,3072]{1,0:T(8,128)(2,1)} %get-tuple-element.6) | data formatting | bytes 786432

commit v4 on v3

--- a/solution.py
+++ b/solution.py
@@ -79,7 +79,7 @@
     q, k, v, m, w,
     out, k_all, v_all, w_all,
     q_here, k_here, v_here, w_here, m_in, bias, query, acc, top_at, total_at,
-    o, stat, o_in, stat_in, ready, mixed_in, mixed, result,
+    o, stat, o_in, stat_in, o_chip, stat_chip, o_far, stat_far, ready, mixed_in, mixed, result,
     send_sems, recv_sems, local_sems,
 ):
     x_hi, z, core, x_lo, y = place()
@@ -273,34 +273,48 @@
 
         lax.fori_loop(0, 1 if second is None else 2, one_block, 0)
 
+    def blended(parts):
+        best = functools.reduce(jnp.maximum, [st[0:1, :] for _, st in parts])
+        shares = [st[1:2, :] * jnp.exp2(st[0:1, :] - best) for _, st in parts]
+        total = functools.reduce(jnp.add, shares)
+        safe = jnp.maximum(total, 1e-30)
+        mean = functools.reduce(
+            jnp.add, [part.astype(jnp.float32) * (one / safe) for (part, _), one in zip(parts, shares)]
+        )
+        return mean, best, total
+
     def partial_out(head):
         mean = (acc[head] / jnp.maximum(total_at[head], 1e-30)).astype(jnp.bfloat16)
         for s in range(slots):
             cols = slice(s * slab, (s + 1) * slab)
-            o[head, s] = mean[:, cols]
-            stat[head, s, 0:1, :] = top_at[head, :, cols]
-            stat[head, s, 1:2, :] = total_at[head, :, cols]
-        arrivals = []
-        for peer_slot, peer in ((across_slot, across), (diagonal_slot, diagonal), (sibling_slot, sibling)):
-            arrivals.append(wires.push(o.at[head, peer_slot], o_in.at[head, slot], peer, o_in.at[head, peer_slot]))
-            arrivals.append(
-                wires.push(stat.at[head, peer_slot], stat_in.at[head, slot], peer, stat_in.at[head, peer_slot])
-            )
-        o_in[head, slot] = o[head, slot]
-        stat_in[head, slot] = stat[head, slot]
-        return arrivals
+            o[head, s % 2, s // 2] = mean[:, cols]
+            stat[head, s % 2, s // 2, 0:1, :] = top_at[head, :, cols]
+            stat[head, s % 2, s // 2, 1:2, :] = total_at[head, :, cols]
+        return [
+            wires.push(o.at[head, other_core], o_in.at[head], sibling, o_in.at[head]),
+            wires.push(stat.at[head, other_core], stat_in.at[head], sibling, stat_in.at[head]),
+        ]
+
+    def partial_on(head, arrivals):
+        for arrival in arrivals:
+            arrival.wait_recv()
+        for hi in range(2):
+            mean, best, total = blended(
+                [(o[head, core, hi], stat[head, core, hi]), (o_in[head, hi], stat_in[head, hi])]
+            )
+            o_chip[head, hi] = mean.astype(jnp.bfloat16)
+            stat_chip[head, hi, 0:1, :] = best
+            stat_chip[head, hi, 1:2, :] = total
+        return [
+            wires.push(o_chip.at[head, other_hi], o_far.at[head], across, o_far.at[head]),
+            wires.push(stat_chip.at[head, other_hi], stat_far.at[head], across, stat_far.at[head]),
+        ]
 
     def partial_in(head, arrivals):
         for arrival in arrivals:
             arrival.wait_recv()
-        tops = [stat_in[head, s, 0:1, :] for s in range(slots)]
-        best = functools.reduce(jnp.maximum, tops)
-        shares = [stat_in[head, s, 1:2, :] * jnp.exp2(tops[s] - best) for s in range(slots)]
-        total = functools.reduce(jnp.add, shares)
-        blend = functools.reduce(
-            jnp.add, [o_in[head, s].astype(jnp.float32) * (shares[s] / total) for s in range(slots)]
-        )
-        ready[head] = blend.T.astype(jnp.bfloat16)
+        mean, _, _ = blended([(o_chip[head, x_hi], stat_chip[head, x_hi]), (o_far[head], stat_far[head])])
+        ready[head] = mean.T.astype(jnp.bfloat16)
         my_lanes = pl.ds(pl.multiple_of(group * HEAD_DIM, HEAD_DIM), HEAD_DIM)
         pieces = []
         for step in range(1, 8):
@@ -357,6 +371,7 @@
     w_far = w_along(y_far, y_far, mine)
     acc[...] = jnp.zeros_like(acc)
     stat[...] = jnp.zeros_like(stat)
+    stat_chip[...] = jnp.zeros_like(stat_chip)
     top_at[...] = jnp.full_like(top_at, LOW)
     total_at[...] = jnp.zeros_like(total_at)
     for arrival in m_wait:
@@ -385,6 +400,12 @@
         work(head, ring_turn(head, 4), (z + 4) % NZ)
         partial.append(partial_out(head))
     turn = ring_turn(heads - 1, 4)
+    partial[0] = partial_on(0, partial[0])
+    work(heads - 1, turn, (z + 4) % NZ)
+    partial.append(partial_out(heads - 1))
+    partial[1] = partial_on(1, partial[1])
+    pieces = [partial_in(0, partial[0])]
+    partial[2] = partial_on(2, partial[2])
     for arrivals in w_crossed:
         for arrival in arrivals:
             arrival.wait_recv()
@@ -394,9 +415,6 @@
         for owner, source in [(group, w.at[:, mine])] + [(g, w_all.at[g]) for g in head_peers]:
             to_band = pl.ds(pl.multiple_of(owner * HEAD_DIM, HEAD_DIM), HEAD_DIM)
             w_loads.append(wires.local(source.at[band, :], w_here.at[head, to_band, :]))
-    pieces = [partial_in(0, partial[0])]
-    work(heads - 1, turn, (z + 4) % NZ)
-    partial.append(partial_out(heads - 1))
     pieces.append(partial_in(1, partial[1]))
     shared = [share(0, pieces[0])]
     pieces.append(partial_in(2, partial[2]))
@@ -456,10 +474,14 @@
             vmem((heads, HEAD_DIM, q_count), f32),
             vmem((heads, 1, q_count), f32),
             vmem((heads, 1, q_count), f32),
-            vmem((heads, slots, HEAD_DIM, slab), bf16),
-            vmem((heads, slots, 8, slab), f32),
-            vmem((heads, slots, HEAD_DIM, slab), bf16),
-            vmem((heads, slots, 8, slab), f32),
+            vmem((heads, 2, 2, HEAD_DIM, slab), bf16),
+            vmem((heads, 2, 2, 8, slab), f32),
+            vmem((heads, 2, HEAD_DIM, slab), bf16),
+            vmem((heads, 2, 8, slab), f32),
+            vmem((heads, 2, HEAD_DIM, slab), bf16),
+            vmem((heads, 2, 8, slab), f32),
+            vmem((heads, HEAD_DIM, slab), bf16),
+            vmem((heads, 8, slab), f32),
             vmem((heads, slab, HEAD_DIM), bf16),
             vmem((heads, 2, 2 * rows, 8 * HEAD_DIM), bf16),
             vmem((4 * rows, quarter), f32),

time: 120 us -> 111 us (0.925)
  Pallas kernels: 118 us -> 109 us
    pallas_call x1, Pallas kernels: 118 us -> 109 us  [body(): pl.pallas_call(fused_kernel, out_shape=[jax.ShapeDtypeStruct(queries.shap...]
where the time goes in v4:
time: 111 us
  Pallas kernels  109 us (98%)
  local copies, waits for them, and re-layouts  1.77 us (2%)
    pallas_call x1, Pallas kernels, body(): pl.pallas_call(fused_kernel, out_shape=[jax.ShapeDtypeStruct(queries.shap...  109 us

profile of v4, /device:TPU:1, one launch (start us, length us, event | category | flops | bytes accessed | tf_op | source)
XLA Modules:
  0.0 110.8 jit_solution(6008150145106377667)
XLA Ops:
  0.0 109.0 %fused.1 = (bf16[64,3072]{1,0:T(8,128)(2,1)}, bf16[3,8,512,128]{3,2,1,0:T(8,128)(2,1)}, bf16[3,8,512,128]{3,2,1,0:T(8,128)(2,1)}, bf16[8,384,768]{2,1,0:T(8,128)(2,1)}) custom-call(bf16[64,3072]{1,0:T(8,128)(2,1)} %q.1, bf16[64,3072]{1,0:T(8,128)(2,1)} %k.1, bf16[64,3072]{1,0:T(8,128)(2,1)} %v.1, s32[3,4,128]{2,1,0:T(4,128)} %m.1, bf16[384,3072]{1,0:T(8,128)(2,1)} %w.1), custom_call_target="tpu_custom_call" | custom-call | tf_op jit(solution)/shard_map/fused/pallas_call | solution.py:456
  109.0 1.8 %copy.7 = bf16[64,3072]{1,0:T(8,128)(2,1)} copy(bf16[64,3072]{1,0:T(8,128)(2,1)} %get-tuple-element.6) | data formatting | bytes 786432

commit v5 on v4

--- a/solution.py
+++ b/solution.py
@@ -358,8 +358,8 @@
         wires.push(m, m_in.at[slot], diagonal, m_in.at[diagonal_slot]),
     ]
     m_own = wires.local(m, m_in.at[slot])
+    own = [ring_start(0)]
     exchange_head(1)
-    own = [ring_start(0)]
     queries_out(0)
     exchange_head(2)
     own.append(ring_start(1))

time: 111 us -> 114 us (1.027)
  Pallas kernels: 109 us -> 112 us
    pallas_call x1, Pallas kernels: 109 us -> 112 us  [body(): pl.pallas_call(fused_kernel, out_shape=[jax.ShapeDtypeStruct(queries.shap...]
where the time goes in v5:
time: 114 us; the launch traced here: 113 us
  Pallas kernels  112 us (98%)
  local copies, waits for them, and re-layouts  1.77 us (2%)
    pallas_call x1, Pallas kernels, body(): pl.pallas_call(fused_kernel, out_shape=[jax.ShapeDtypeStruct(queries.shap...  112 us

profile of v5, /device:TPU:1, one launch (start us, length us, event | category | flops | bytes accessed | tf_op | source)
XLA Modules:
  0.0 113.4 jit_solution(4608548653700016111)
XLA Ops:
  0.0 111.6 %fused.1 = (bf16[64,3072]{1,0:T(8,128)(2,1)}, bf16[3,8,512,128]{3,2,1,0:T(8,128)(2,1)}, bf16[3,8,512,128]{3,2,1,0:T(8,128)(2,1)}, bf16[8,384,768]{2,1,0:T(8,128)(2,1)}) custom-call(bf16[64,3072]{1,0:T(8,128)(2,1)} %q.1, bf16[64,3072]{1,0:T(8,128)(2,1)} %k.1, bf16[64,3072]{1,0:T(8,128)(2,1)} %v.1, s32[3,4,128]{2,1,0:T(4,128)} %m.1, bf16[384,3072]{1,0:T(8,128)(2,1)} %w.1), custom_call_target="tpu_custom_call" | custom-call | tf_op jit(solution)/shard_map/fused/pallas_call | solution.py:456
  111.6 1.8 %copy.7 = bf16[64,3072]{1,0:T(8,128)(2,1)} copy(bf16[64,3072]{1,0:T(8,128)(2,1)} %get-tuple-element.6) | data formatting | bytes 786432
